TPU v7x, 512 devices: a whole 4x4x16 slice. The times are simulated.
512 devices in a mesh: expert: 128 (over z, x, core), hidden: 4 (over y).
Axes of the slice: x: 4, y: 4, z: 16, core: 2. Of those that a mesh axis runs over, the one named last changes fastest.
Arguments:
- tokens: bfloat16 [2048, 4096], P('expert', 'hidden'), may hold values from -6 to 6
- expert_ids: int32 [2048, 8], P('expert'), may hold values from 0 to 127, all different within a row; in each aligned block of 16 rows (0 to 15, 16 to 31, ...) at most 2 rows name the same one
- route_probs: float32 [2048, 8], P('expert'), may hold values from 0.02 to 1
- gate_weight: bfloat16 [128, 768, 4096], P('expert', 'hidden'), may hold values from -0.09375 to 0.09375
- up_weight: bfloat16 [128, 768, 4096], P('expert', 'hidden'), may hold values from -0.09375 to 0.09375
- down_weight: bfloat16 [128, 768, 4096], P('expert', 'hidden'), may hold values from -0.21875 to 0.21875
Outputs:
- layer_out: bfloat16 [2048, 4096], P('expert', 'hidden')
Inputs may be any that keep to these rules, and one draw needn't show every extreme that they name: `expert_ids`: among the 16 tokens of one index of the expert axis no expert is named more than 2 times, a bound that some block reaches; a token's 8 ids differ.
All inputs are finite; a program needn't handle non-finite values.
Results may differ from a plain program's by a relative error of at most 0.015.
Values may be sent and summed in bfloat16 or wider, within the bound.
A program may use at most 64 MiB of HBM per device.

v0:
```python
import jax
import jax.numpy as jnp
from jax import lax
from jax.sharding import PartitionSpec as P


def slot_layout(expert_ids, experts, capacity):
    flat_ids = expert_ids.reshape(-1)
    onehot = (flat_ids[:, None] == jnp.arange(experts, dtype=jnp.int32)[None, :]).astype(jnp.int32)
    arrival = jnp.sum((jnp.cumsum(onehot, axis=0) - 1) * onehot, axis=1)
    slot_index = (flat_ids * capacity + arrival).reshape(expert_ids.shape)
    select = (
        slot_index[:, :, None] == jnp.arange(experts * capacity, dtype=jnp.int32)[None, None, :]
    ).any(axis=1)
    return (slot_index, select.astype(jnp.bfloat16))


def per_device(tokens, expert_ids, route_probs, gate_weight, up_weight, down_weight):
    experts = lax.axis_size("expert")
    token_count, top_count = expert_ids.shape
    capacity = min(token_count, 2 * token_count * top_count // experts)
    weights = route_probs / jnp.sum(route_probs, axis=1, keepdims=True)
    slot_index, select = slot_layout(expert_ids, experts, capacity)
    width = gate_weight.shape[2]
    full_tokens = lax.all_gather(tokens, "hidden", axis=1, tiled=True)
    outgoing = jnp.dot(select.T, full_tokens, preferred_element_type=jnp.float32).astype(
        jnp.bfloat16
    )
    arrived = lax.all_to_all(
        outgoing.reshape(experts, capacity, width),
        "expert",
        split_axis=0,
        concat_axis=0,
        tiled=True,
    )
    row_data = arrived.reshape(experts * capacity, width)
    contract = (((1,), (1,)), ((), ()))
    gate_out = lax.dot_general(
        row_data, gate_weight[0], contract, preferred_element_type=jnp.float32
    )
    up_out = lax.dot_general(row_data, up_weight[0], contract, preferred_element_type=jnp.float32)
    activated = (jax.nn.silu(gate_out) * up_out).astype(jnp.bfloat16)
    partial_out = jnp.dot(activated, down_weight[0], preferred_element_type=jnp.float32)
    summed = lax.psum_scatter(
        partial_out.reshape(experts, capacity, width).astype(jnp.bfloat16),
        "hidden",
        scatter_dimension=2,
        tiled=True,
    ).astype(jnp.float32)
    returned = lax.all_to_all(
        summed.astype(jnp.bfloat16), "expert", split_axis=0, concat_axis=0, tiled=True
    ).astype(summed.dtype)
    picked = returned.reshape(experts * capacity, tokens.shape[1])[slot_index]
    combined = jnp.sum(weights[:, :, None] * picked, axis=1)
    return combined.astype(jnp.bfloat16)


def solution(mesh):
    placed = (
        P("expert", "hidden"),
        P("expert", None),
        P("expert", None),
        P("expert", "hidden", None),
        P("expert", "hidden", None),
        P("expert", "hidden", None),
    )
    return jax.shard_map(
        per_device, mesh=mesh, in_specs=placed, out_specs=P("expert", "hidden"), check_vma=False
    )
```

profile of v0, /device:TPU:1, one launch (start us, length us, event | category | flops | bytes accessed | tf_op | source)
XLA Modules:
  0.0 245.0 jit_solution(9247400619854694511)
XLA Ops:
  6.5 0.0 copy-start
  6.5 0.0 reduce-scatter.2.cloned.1.call-start
  6.5 0.9 copy.24
  7.4 0.1 eq.28
  7.5 0.1 fusion.14
  7.6 0.2 reduce_window_sum.11
  7.8 0.2 select_reduce_fusion
  7.9 0.1 reduce_sum.31
  8.1 0.1 fusion.13
  8.2 10.7 %all_gather.3 = bf16[16,4096]{1,0:T(8,128)(2,1)S(1)} all-gather(bf16[16,1024]{1,0:T(8,128)(2,1)} %param.6), channel_id=1, replica_groups=mesh['expert'=128,'hidden'=4] {'hidden'}, dimensions={1}, use_global_device_ids=true | all-gather | bytes 163840 | tf_op jit(solution)/shard_map/all_gather | solution.py:25
  18.8 2.0 convolution_convert_fusion.1
  20.9 4.4 %reshape.26 = bf16[128,2,4096]{2,1,0:T(2,128)(2,1)} reshape(bf16[256,4096]{1,0:T(8,128)(2,1)} %convolution_convert_fusion.1) | data formatting | bytes 4194304 | tf_op jit(solution)/shard_map/reshape | solution.py:30
  25.3 119.4 %all_to_all.10 = bf16[128,2,4096]{2,1,0:T(2,128)(2,1)} all-to-all(bf16[128,2,4096]{2,1,0:T(2,128)(2,1)} %reshape.26), channel_id=1, replica_groups=mesh['expert'=128,'hidden'=4] {'expert'}, dimensions={0} | all-to-all | bytes 4194304 | tf_op jit(solution)/shard_map/all_to_all | solution.py:29
  144.7 4.2 %reshape.27 = bf16[256,4096]{1,0:T(8,128)(2,1)} reshape(bf16[128,2,4096]{2,1,0:T(2,128)(2,1)} %all_to_all.10) | data formatting | bytes 4194304 | tf_op jit(solution)/shard_map/reshape | solution.py:36
  148.9 0.0 copy-done.2
  148.9 2.6 %fusion.3 = f32[256,192]{0,1:T(8,128)S(1)} fusion(bf16[256,4096]{1,0:T(8,128)(2,1)} %reshape.27, bf16[1,192,4096]{2,1,0:T(8,128)(2,1)S(1)} %copy-done.2), kind=kOutput, calls=%fused_computation.6 | convolution fusion | flops 402653184 | bytes 3866624 | tf_op jit(solution)/shard_map/dot_general | solution.py:38
  151.6 0.1 copy-done.4
  151.6 0.8 fusion.8
  152.5 0.1 copy.26
  152.6 0.1 dot_general.17
  152.7 0.0 copy-done
  152.7 2.1 convolution_convert_fusion
  154.7 0.0 reduce-scatter.2.cloned.1.call-update
  154.7 31.9 %reduce-scatter.2.cloned.1.call-done = bf16[128,2,1024]{2,0,1:T(8,128)(2,1)} async-done(((bf16[128,2,4096]{2,0,1:T(8,128)(2,1)}), bf16[128,2,1024]{2,0,1:T(8,128)(2,1)}) %reduce-scatter.2.cloned.1.call-update) | async-done | bytes 524304 | tf_op jit(solution)/shard_map/reduce_scatter | solution.py:44
  186.6 2.4 copy.28
  189.0 16.6 %all-to-all-start.1 = ((bf16[128,2,1024]{2,1,0:T(2,128)(2,1)}), bf16[128,2,1024]{2,1,0:T(2,128)(2,1)S(1)}, u32[]{:S(2)}, u32[]{:S(2)}) async-start(bf16[128,2,1024]{2,1,0:T(2,128)(2,1)} %copy.28), calls=%async_computation.2 | async-start | bytes 1048576 | tf_op jit(solution)/shard_map/all_to_all | solution.py:50
  205.5 0.1 reshape.34
  205.7 0.1 copy.23
  205.8 30.6 %all-to-all-done.1 = bf16[128,2,1024]{2,1,0:T(2,128)(2,1)S(1)} async-done(((bf16[128,2,1024]{2,1,0:T(2,128)(2,1)}), bf16[128,2,1024]{2,1,0:T(2,128)(2,1)S(1)}, u32[]{:S(2)}, u32[]{:S(2)}) %all-to-all-start.1) | async-done | bytes 524320 | tf_op jit(solution)/shard_map/all_to_all | solution.py:50
  236.4 0.1 reshape.31
  236.5 0.8 gather_fusion
  237.3 0.8 fusion.11
  (10 shorter events, 0.1 us)
Async XLA Ops:
  6.5 146.1 %copy-start = (bf16[1,192,4096]{2,1,0:T(8,128)(2,1)S(1)}, bf16[1,192,4096]{2,1,0:T(8,128)(2,1)}, u32[]{:S(2)}) copy-start(bf16[1,192,4096]{2,1,0:T(8,128)(2,1)} %param.11) | copy-start | bytes 4718596
  6.5 180.1 %reduce-scatter.2.cloned.1.call-start = ((), (), s32[]{:S(2)}) async-start(), calls=%async_computation.3 | async-start | bytes 2621440 | tf_op jit(solution)/shard_map/reduce_scatter | solution.py:44
  144.7 4.2 %copy-start.2 = (bf16[1,192,4096]{2,1,0:T(8,128)(2,1)S(1)}, bf16[1,192,4096]{2,1,0:T(8,128)(2,1)}, u32[]{:S(2)}) copy-start(bf16[1,192,4096]{2,1,0:T(8,128)(2,1)} %param.9) | copy-start | bytes 4718596
  148.9 2.6 %copy-start.1 = (bf16[256,4096]{1,0:T(8,128)(2,1)S(1)}, bf16[256,4096]{1,0:T(8,128)(2,1)}, u32[]{:S(2)}) copy-start(bf16[256,4096]{1,0:T(8,128)(2,1)} %reshape.27) | copy-start | bytes 6291460
  148.9 2.7 %copy-start.4 = (bf16[1,192,4096]{2,1,0:T(8,128)(2,1)S(1)}, bf16[1,192,4096]{2,1,0:T(8,128)(2,1)}, u32[]{:S(2)}) copy-start(bf16[1,192,4096]{2,1,0:T(8,128)(2,1)} %param.10) | copy-start | bytes 4718596
  154.7 50.9 %copy-start.3 = (f32[16,8]{0,1:T(8,128)S(1)}, f32[16,8]{0,1:T(8,128)}, u32[]{:S(2)}) copy-start(f32[16,8]{0,1:T(8,128)} %param.8) | copy-start | bytes 1540
  189.0 47.4 %all-to-all-start.1 = ((bf16[128,2,1024]{2,1,0:T(2,128)(2,1)}), bf16[128,2,1024]{2,1,0:T(2,128)(2,1)S(1)}, u32[]{:S(2)}, u32[]{:S(2)}) async-start(bf16[128,2,1024]{2,1,0:T(2,128)(2,1)} %copy.28), calls=%async_computation.2 | async-start | bytes 1048576 | tf_op jit(solution)/shard_map/all_to_all | solution.py:50
Sparse Core Ops, SparseCore 0:
  154.9 31.6 reduce-scatter.1
where the time goes:
time: 247 us; the launch traced here: 245 us
  blocking collectives  130 us (53%)
  waiting for transfers between devices  62.5 us (25%)
  starting transfers between devices  16.6 us (7%)
  between operations  13.5 us (5%)
  local copies, waits for them, and re-layouts  13.4 us (5%)
  matrix products  7.53 us (3%)
    all_to_all x1, blocking collectives, per_device(): lax.all_to_all(outgoing.reshape(experts, capacity, width), 'expert', spli...  119 us
    reduce_scatter x1, waiting for transfers between devices, per_device(): lax.psum_scatter(partial_out.reshape(experts, capacity, width).astype(jnp...  31.9 us
    all_to_all x1, waiting for transfers between devices, per_device(): lax.all_to_all(summed.astype(jnp.bfloat16), 'expert', split_axis=0, conca...  30.6 us
    all_to_all x1, starting transfers between devices, per_device(): lax.all_to_all(summed.astype(jnp.bfloat16), 'expert', split_axis=0, conca...  16.6 us
    all_gather x1, blocking collectives, per_device(): full_tokens = lax.all_gather(tokens, 'hidden', axis=1, tiled=True)  10.7 us
  transfers between devices with their start and end apart: 2, of which 2 were waited for; matrix products, arithmetic and copies ran while one was open for 0% of the time, Pallas kernels for 0%

commit v1 on v0

v1 whole, which is shorter than its diff:
```python
import jax
import jax.numpy as jnp
from jax import lax
from jax.experimental import pallas as pl
from jax.experimental.pallas import tpu as pltpu
from jax.sharding import PartitionSpec as P

MESH = pl.DeviceIdType.MESH
BF16 = jnp.bfloat16
F32 = jnp.float32
NZ, NXC, NY = 16, 8, 4
NEAR = 32
GROUPS = ((0,), (1,), (3,), (2,))
BASE = (0, 64, 128, 192)
ROWS = (64, 64, 64, 64)
EXPERT = ((0,), (1,), (2,), (3,))
ORDER = (
    ("h", 0), ("a", 0), ("p", 0), ("b", 0), ("a", 1), ("a", 2), ("c", 0), ("b", 1), ("a", 3), ("b", 2),
    ("c", 1), ("w", 0), ("b", 3), ("c", 2), ("d", 1), ("c", 3), ("d", 2), ("e", 1), ("d", 3), ("e", 2),
    ("f", 1), ("d", 0), ("e", 3), ("f", 2), ("e", 0), ("f", 3), ("g", 1), ("g", 2), ("f", 0), ("g", 3),
    ("g", 0),
)


def kernel(tok_hbm, ids_hbm, prob_hbm, gate_hbm, up_hbm, down_hbm, out_ref, *scratch):
    (tok, ids_ref, prob_ref, gate, up, down, far, wanted, perm, perm_back, weighted, xf, pf, step1, step2,
     part_out, part_in, in_sem, far_s, far_r, near_s, near_r, y_s, y_r, one_s, one_r, two_s, two_r,
     back_s, back_r, part_s, part_r) = scratch[:32]
    n = len(GROUPS)
    picked, got, back_out, back_in = (scratch[32 + n * i : 32 + n * i + n] for i in range(4))

    e = lax.axis_index("expert")
    y = lax.axis_index("hidden")
    z, xc = lax.div(e, NXC), lax.rem(e, NXC)
    two = jnp.where(lax.rem(z, 4) < 2, 2, NZ - 2)

    def along_y(dy):
        return (e, lax.rem(y + dy, NY))

    def along_z(dz):
        return (lax.rem(z + dz, NZ) * NXC + xc, y)

    z_bases = [lax.rem(z + dz, NZ) * NXC for dz in (0, 1, NZ - 1, two)]
    xcs = [lax.rem(xc + d, NXC) for d in range(NXC)]

    def ahead(j):
        return (z_bases[j // 8] + xcs[j % 8], y)

    def behind(j):
        return (z_bases[(0, 2, 1, 3)[j // 8]] + xcs[-j % 8], y)

    barrier = pltpu.get_barrier_semaphore()
    partners = [along_z(4 * k) for k in (1, 3, 2)]
    partners += [ahead(j) for j in range(NEAR - 1, 0, -1)]
    partners += [along_y(k) for k in range(1, NY)]
    inputs = [
        pltpu.make_async_copy(src, dst, in_sem.at[i])
        for i, (src, dst) in enumerate((
            (tok_hbm, tok), (ids_hbm, ids_ref), (prob_hbm, prob_ref),
            (gate_hbm.at[0], gate), (up_hbm.at[0], up), (down_hbm.at[0], down),
        ))
    ]
    for i in range(3):
        inputs[i].start()
    for partner in partners:
        pl.semaphore_signal(barrier, inc=1, device_id=partner, device_id_type=MESH)

    def remote(src, dst, send, recv, device):
        copy = pltpu.make_async_remote_copy(
            src_ref=src, dst_ref=dst, send_sem=send, recv_sem=recv,
            device_id=device, device_id_type=MESH,
        )
        copy.start()
        return copy

    def iota(shape, axis):
        return lax.broadcasted_iota(jnp.int32, shape, axis)

    nt = (((1,), (1,)), ((), ()))

    for i in range(3):
        inputs[i].wait()
    for group in range(8):
        far[0, 16 * group : 16 * group + 16, :] = tok[:, 128 * group : 128 * group + 128]
    probs = prob_ref[...]
    share = probs / jnp.sum(probs, axis=0, keepdims=True)
    lists = jnp.concatenate([ids_ref[...].astype(F32), share, jnp.zeros((112, 16), F32)], axis=0).astype(BF16)
    same = (iota((16, 16), 0) == iota((16, 16), 1)).astype(F32).astype(BF16)
    far[0, 128:144, :] = lax.dot_general(same, lists, nt, preferred_element_type=F32).astype(BF16)

    pl.semaphore_wait(barrier, len(partners))

    far_copies = {}

    def send_far(_):
        for k in (1, 3, 2):
            far_copies[k] = remote(far.at[0], far.at[k], far_s.at[k], far_r.at[k], along_z(4 * k))

    for i in range(3, 6):
        inputs[i].start()

    row, col = iota((512, 256), 0), iota((512, 256), 1)
    hop = row >> 7
    dz = jnp.where(hop == 0, 0, jnp.where(hop == 1, 1, jnp.where(hop == 2, NZ - 1, two)))
    target = ((z + dz) & 15) * NXC + ((xc + (row >> 4)) & 7) + ((row & 1) << 7)
    wanted[...] = (target == col).astype(F32).astype(BF16)
    same_group = ((iota((512, 128), 0) & 15) >> 1) == (iota((512, 128), 1) >> 4)

    lane = iota((16, 128), 1).astype(F32)
    below = (iota((16, 16), 0) > iota((16, 16), 1)).astype(F32).astype(BF16)

    def turns(k, weigh):
        lists = far[k, 128:144, :].astype(F32)
        named, value = jnp.zeros((16, 128), F32), jnp.zeros((16, 128), F32)
        for q in range(8):
            hit = lists[:, q : q + 1] == lane
            named = jnp.where(hit, 1.0, named)
            if weigh:
                value = jnp.where(hit, lists[:, 8 + q : 9 + q], value)
        rank = jnp.dot(below, named.astype(BF16), preferred_element_type=F32)
        what = value if weigh else named
        return jnp.concatenate([jnp.where(rank == 0.0, what, 0.0), jnp.where(rank == 1.0, what, 0.0)], axis=1)

    def spread(block):
        return jnp.concatenate([block] * 8, axis=0).astype(BF16)

    def select_and_send(g):
        for i, k in enumerate(GROUPS[g]):
            if k:
                far_copies[k].wait_recv()
            chosen = lax.dot_general(wanted[...], spread(turns(k, False)), nt, preferred_element_type=F32)
            chosen = jnp.where(same_group, chosen, 0.0).astype(BF16)
            picked[g][:, 128 * i : 128 * i + 128] = jnp.dot(
                chosen, far[k, 0:128, :], preferred_element_type=F32
            ).astype(BF16)
        for j in range(NEAR - 1, 0, -1):
            remote(
                picked[g].at[pl.ds(16 * j, 16)], got[g].at[pl.ds(16 * j, 16)],
                near_s.at[g], near_r.at[g], ahead(j),
            )
        got[g][0:16, :] = picked[g][0:16, :]

    def permutations(_):
        a, b = iota((512, 512), 0), iota((512, 512), 1)
        perm[...] = (b == (((a & 63) >> 1) << 4) + ((a >> 6) << 1) + (a & 1)).astype(F32).astype(BF16)
        perm_back[...] = (a == (((b & 63) >> 1) << 4) + ((b >> 6) << 1) + (b & 1)).astype(F32).astype(BF16)

    def weights(_):
        for i in range(3, 6):
            inputs[i].wait()
        same = (iota((128, 512), 0) >> 4) == ((iota((128, 512), 1) & 15) >> 1)
        for k in range(4):
            full = lax.dot_general(spread(turns(k, True)), wanted[...], nt, preferred_element_type=F32)
            weighted[k] = jnp.where(same, full, 0.0).astype(BF16)

    def wait_all(ref, sem):
        rest = ref.at[pl.ds(16, 496)]
        pltpu.make_async_copy(rest, rest, sem).wait()

    y_copies, one_copies, two_copies, part_copies = {}, {}, {}, {}

    def send_y(g):
        wait_all(got[g], near_r.at[g])
        rows = jnp.dot(perm[...], got[g][...], preferred_element_type=F32).astype(BF16)
        for i in range(len(GROUPS[g])):
            first = BASE[g] + 64 * i
            for group in range(8):
                xf[y, first : first + 64, 128 * group : 128 * group + 128] = rows[
                    64 * group : 64 * group + 64, 128 * i : 128 * i + 128
                ]
        block = xf.at[y, pl.ds(BASE[g], ROWS[g])]
        y_copies[g, 0] = remote(block, block, y_s.at[g, 0], y_r.at[g, 0], along_y(1))
        y_copies[g, 1] = remote(block, block, y_s.at[g, 1], y_r.at[g, 1], along_y(3))

    def first_half(g):
        return pl.ds(BASE[g], ROWS[g] // 2)

    def second_half(g):
        return pl.ds(BASE[g] + ROWS[g] // 2, ROWS[g] // 2)

    def forward_y(g):
        y_copies[g, 0].wait_recv()
        block = xf.at[lax.rem(y + 3, NY), first_half(g)]
        y_copies[g, 2] = remote(block, block, y_s.at[g, 2], y_r.at[g, 2], along_y(1))
        y_copies[g, 1].wait_recv()
        block = xf.at[lax.rem(y + 1, NY), second_half(g)]
        y_copies[g, 3] = remote(block, block, y_s.at[g, 3], y_r.at[g, 3], along_y(3))

    def expert(which):
        members = EXPERT[which]
        for g in members:
            y_copies[g, 2].wait_recv()
            y_copies[g, 3].wait_recv()
        count = sum(ROWS[g] for g in members)
        rows = pl.ds(BASE[members[0]], count)
        gate_out, up_out = jnp.zeros((count, 192), F32), jnp.zeros((count, 192), F32)
        for q in range(NY):
            x = xf[q, rows, :]
            gate_out += lax.dot_general(x, gate[:, 1024 * q : 1024 * q + 1024], nt, preferred_element_type=F32)
            up_out += lax.dot_general(x, up[:, 1024 * q : 1024 * q + 1024], nt, preferred_element_type=F32)
        hidden = (gate_out / (1.0 + jnp.exp(-gate_out)) * up_out).astype(BF16)
        for q in range(NY):
            pf[q, rows, :] = jnp.dot(
                hidden, down[:, 1024 * q : 1024 * q + 1024], preferred_element_type=F32
            ).astype(BF16)
        opposite = lax.rem(y + 2, NY)
        for g in members:
            for side, half, dy in ((0, first_half(g), 1), (1, second_half(g), 3)):
                one_copies[g, side] = remote(
                    pf.at[opposite, half], step1.at[half], one_s.at[g, side], one_r.at[g, side], along_y(dy)
                )

    def add_y(g):
        for side, half, dy in ((0, first_half(g), 1), (1, second_half(g), 3)):
            one_copies[g, side].wait_recv()
            to = lax.rem(y + dy, NY)
            pf[to, half, :] = (pf[to, half, :].astype(F32) + step1[half, :].astype(F32)).astype(BF16)
            rows = pl.ds(BASE[g], ROWS[g])
            two_copies[g, side] = remote(
                pf.at[to, rows], step2.at[side, rows], two_s.at[g, side], two_r.at[g, side], along_y(dy)
            )

    def give_back(g):
        two_copies[g, 0].wait_recv()
        two_copies[g, 1].wait_recv()
        parts = []
        for i in range(len(GROUPS[g])):
            rows = pl.ds(BASE[g] + 64 * i, 64)
            total = (
                pf[y, rows, :].astype(F32) + step2[0, rows, :].astype(F32) + step2[1, rows, :].astype(F32)
            ).astype(BF16)
            parts.append(
                jnp.concatenate([total[:, 128 * group : 128 * group + 128] for group in range(8)], axis=0)
            )
        stacked = jnp.concatenate(parts, axis=1) if len(parts) > 1 else parts[0]
        back_out[g][...] = jnp.dot(perm_back[...], stacked, preferred_element_type=F32).astype(BF16)
        for j in range(NEAR - 1, 0, -1):
            remote(
                back_out[g].at[pl.ds(16 * j, 16)], back_in[g].at[pl.ds(16 * j, 16)],
                back_s.at[g], back_r.at[g], behind(j),
            )
        back_in[g][0:16, :] = back_out[g][0:16, :]

    own = []

    def combine(g):
        wait_all(back_in[g], back_r.at[g])
        for i, k in enumerate(GROUPS[g]):
            part = jnp.dot(weighted[k], back_in[g][:, 128 * i : 128 * i + 128], preferred_element_type=F32)
            if k == 0:
                own.append(part)
            else:
                part_out[k] = part.astype(BF16)
                part_copies[k] = remote(
                    part_out.at[k], part_in.at[k], part_s.at[k], part_r.at[k], along_z(NZ - 4 * k)
                )

    stages = {
        "a": select_and_send, "p": permutations, "b": send_y, "c": forward_y, "w": weights,
        "h": send_far, "d": expert, "e": add_y, "f": give_back, "g": combine,
    }
    for stage, g in ORDER:
        stages[stage](g)

    result = own[0]
    for k in (1, 3, 2):
        part_copies[k].wait_recv()
        result += part_in[k].astype(F32)
    for group in range(8):
        out_ref[:, 128 * group : 128 * group + 128] = result[16 * group : 16 * group + 16, :].astype(BF16)

    for g in range(len(GROUPS)):
        wait_all(picked[g], near_s.at[g])
        wait_all(back_out[g], back_s.at[g])
        for i in range(4):
            y_copies[g, i].wait_send()
        for i in range(2):
            one_copies[g, i].wait_send()
            two_copies[g, i].wait_send()
    for k in range(1, 4):
        far_copies[k].wait_send()
        part_copies[k].wait_send()


def per_device(tokens, expert_ids, route_probs, gate_weight, up_weight, down_weight):
    vmem, dma = pltpu.VMEM, pltpu.SemaphoreType.DMA
    in_hbm = pl.BlockSpec(memory_space=pltpu.HBM)
    n = len(GROUPS)
    messages = [vmem((512, 128 * len(members)), BF16) for members in GROUPS]
    return pl.pallas_call(
        kernel,
        out_shape=jax.ShapeDtypeStruct((16, 1024), BF16),
        in_specs=[in_hbm] * 6,
        out_specs=pl.BlockSpec(memory_space=pltpu.VMEM),
        scratch_shapes=[
            vmem((16, 1024), BF16), vmem((8, 16), jnp.int32), vmem((8, 16), F32),
            vmem((192, 4096), BF16), vmem((192, 4096), BF16), vmem((192, 4096), BF16),
            vmem((4, 144, 128), BF16),
            vmem((512, 256), BF16), vmem((512, 512), BF16), vmem((512, 512), BF16),
            vmem((4, 128, 512), BF16),
            vmem((4, 256, 1024), BF16), vmem((4, 256, 1024), BF16),
            vmem((256, 1024), BF16), vmem((2, 256, 1024), BF16),
            vmem((4, 128, 128), BF16), vmem((4, 128, 128), BF16),
            dma((6,)), dma((4,)), dma((4,)), dma((n,)), dma((n,)),
            dma((n, 4)), dma((n, 4)), dma((n, 2)), dma((n, 2)), dma((n, 2)), dma((n, 2)),
            dma((n,)), dma((n,)), dma((4,)), dma((4,)),
        ] + messages * 4,
        compiler_params=pltpu.CompilerParams(
            collective_id=0, has_side_effects=True, vmem_limit_bytes=60 * 1024 * 1024
        ),
        cost_estimate=pl.CostEstimate(flops=1_300_000_000, bytes_accessed=5_000_000, transcendentals=50_000),
    )(tokens, expert_ids.T, route_probs.T, gate_weight, up_weight, down_weight)


def solution(mesh):
    placed = (
        P("expert", "hidden"),
        P("expert", None),
        P("expert", None),
        P("expert", "hidden", None),
        P("expert", "hidden", None),
        P("expert", "hidden", None),
    )
    return jax.shard_map(
        per_device, mesh=mesh, in_specs=placed, out_specs=P("expert", "hidden"), check_vma=False
    )
```

time: 247 us -> 80.1 us (0.32)
  blocking collectives: 130 us -> 0 us
  Pallas kernels: 0 us -> 78.4 us
  waiting for transfers between devices: 62.5 us -> 0 us
  starting transfers between devices: 16.6 us -> 0 us
  between operations: 13.5 us -> 0.01 us
  local copies, waits for them, and re-layouts: 13.4 us -> 1.38 us
  matrix products: 7.53 us -> 0 us
    all_to_all x1 -> x0, blocking collectives: 119 us -> none  [per_device(): lax.all_to_all(outgoing.reshape(experts, capacity, width), 'expert', spli...]
    pallas_call x0 -> x1, Pallas kernels: none -> 78.4 us  [per_device(): pl.pallas_call(kernel, out_shape=jax.ShapeDtypeStruct((16, 1024), BF16),...]
    reduce_scatter x1 -> x0, waiting for transfers between devices: 31.9 us -> none  [per_device(): lax.psum_scatter(partial_out.reshape(experts, capacity, width).astype(jnp...]
    all_to_all x1 -> x0, waiting for transfers between devices: 30.6 us -> none  [per_device(): lax.all_to_all(summed.astype(jnp.bfloat16), 'expert', split_axis=0, conca...]
    all_to_all x1 -> x0, starting transfers between devices: 16.6 us -> none  [per_device(): lax.all_to_all(summed.astype(jnp.bfloat16), 'expert', split_axis=0, conca...]
    all_gather x1 -> x0, blocking collectives: 10.7 us -> none  [per_device(): full_tokens = lax.all_gather(tokens, 'hidden', axis=1, tiled=True)]
    reshape x3 -> x0, local copies, waits for them, and re-layouts: 8.77 us -> none  [the longest x1 4.39 us: per_device(): outgoing.reshape(experts, capacity, width)]
    dot_general x4 -> x0, matrix products: 7.53 us -> none  [the longest x1 2.59 us: per_device(): lax.dot_general(row_data, gate_weight[0], contract, preferred_element_typ...]
  transfers between devices with their start and end apart: 2 -> 0, of which waited for: 2 -> 0; matrix products, arithmetic and copies ran while one was open for 0% -> 0% of each run, Pallas kernels for 0% -> 0%
where the time goes in v1:
time: 80.1 us; the launch traced here: 79.8 us
  Pallas kernels  78.4 us (98%)
  local copies, waits for them, and re-layouts  1.38 us (2%)
    pallas_call x1, Pallas kernels, per_device(): pl.pallas_call(kernel, out_shape=jax.ShapeDtypeStruct((16, 1024), BF16),...  78.4 us

profile of v1, /device:TPU:1, one launch (start us, length us, event | category | flops | bytes accessed | tf_op | source)
XLA Modules:
  0.0 79.8 jit_solution(12693495001687290280)
XLA Ops:
  0.0 78.4 %shard_map.64 = bf16[16,1024]{1,0:T(8,128)(2,1)} custom-call(bf16[16,1024]{1,0:T(8,128)(2,1)} %tok_hbm.1, s32[8,16]{1,0:T(8,128)} %bitcast.2, f32[8,16]{1,0:T(8,128)} %bitcast.3, bf16[1,192,4096]{2,1,0:T(8,128)(2,1)} %gate_hbm.1, bf16[1,192,4096]{2,1,0:T(8,128)(2,1)} %up_hbm.1, bf16[1,192,4096]{2,1,0:T(8,128)(2,1)} %down_hbm.1), custom_call_target="tpu_custom_call" | custom-call | flops 1300000000 | bytes 5000000 | tf_op jit(solution)/shard_map/pallas_call | solution.py:290
  78.4 1.4 %copy.8 = bf16[16,1024]{1,0:T(8,128)(2,1)} copy(bf16[16,1024]{1,0:T(8,128)(2,1)} %shard_map.64) | data formatting | bytes 65536

commit v2 on v1

--- a/solution.py
+++ b/solution.py
@@ -14,11 +14,12 @@
 BASE = (0, 64, 128, 192)
 ROWS = (64, 64, 64, 64)
 EXPERT = ((0,), (1,), (2,), (3,))
+MIX = (2,)
 ORDER = (
-    ("h", 0), ("a", 0), ("p", 0), ("b", 0), ("a", 1), ("a", 2), ("c", 0), ("b", 1), ("a", 3), ("b", 2),
-    ("c", 1), ("w", 0), ("b", 3), ("c", 2), ("d", 1), ("c", 3), ("d", 2), ("e", 1), ("d", 3), ("e", 2),
-    ("f", 1), ("d", 0), ("e", 3), ("f", 2), ("e", 0), ("f", 3), ("g", 1), ("g", 2), ("f", 0), ("g", 3),
-    ("g", 0),
+    ("h", 0), ("a", 0), ("p", 0), ("b", 0), ("i", 0), ("a", 1), ("a", 2), ("c", 0), ("b", 1), ("a", 3),
+    ("b", 2), ("c", 1), ("w", 0), ("b", 3), ("c", 2), ("d", 1), ("c", 3), ("d", 2), ("f", 2), ("e", 1),
+    ("d", 3), ("f", 1), ("d", 0), ("e", 3), ("g", 2), ("e", 0), ("g", 1), ("s", 2), ("f", 3), ("f", 0),
+    ("g", 3), ("g", 0),
 )
 
 
@@ -28,11 +29,12 @@
      back_s, back_r, part_s, part_r) = scratch[:32]
     n = len(GROUPS)
     picked, got, back_out, back_in = (scratch[32 + n * i : 32 + n * i + n] for i in range(4))
+    all_out, all_in, all_s, all_r = scratch[32 + 4 * n :]
 
     e = lax.axis_index("expert")
     y = lax.axis_index("hidden")
     z, xc = lax.div(e, NXC), lax.rem(e, NXC)
-    two = jnp.where(lax.rem(z, 4) < 2, 2, NZ - 2)
+    two = jnp.where(lax.rem(xc, 2) == 0, 2, NZ - 2)
 
     def along_y(dy):
         return (e, lax.rem(y + dy, NY))
@@ -41,17 +43,20 @@
         return (lax.rem(z + dz, NZ) * NXC + xc, y)
 
     z_bases = [lax.rem(z + dz, NZ) * NXC for dz in (0, 1, NZ - 1, two)]
+    z_behind = lax.rem(z + NZ - two, NZ) * NXC
     xcs = [lax.rem(xc + d, NXC) for d in range(NXC)]
 
     def ahead(j):
         return (z_bases[j // 8] + xcs[j % 8], y)
 
     def behind(j):
-        return (z_bases[(0, 2, 1, 3)[j // 8]] + xcs[-j % 8], y)
+        base = (z_bases[0], z_bases[2], z_bases[1], z_bases[3] if j % 2 else z_behind)[j // 8]
+        return (base + xcs[-j % 8], y)
 
     barrier = pltpu.get_barrier_semaphore()
-    partners = [along_z(4 * k) for k in (1, 3, 2)]
+    partners = [along_z(4), along_z(12)]
     partners += [ahead(j) for j in range(NEAR - 1, 0, -1)]
+    partners += [(z_behind + xcs[d], y) for d in range(0, NXC, 2)]
     partners += [along_y(k) for k in range(1, NY)]
     inputs = [
         pltpu.make_async_copy(src, dst, in_sem.at[i])
@@ -88,17 +93,6 @@
     same = (iota((16, 16), 0) == iota((16, 16), 1)).astype(F32).astype(BF16)
     far[0, 128:144, :] = lax.dot_general(same, lists, nt, preferred_element_type=F32).astype(BF16)
 
-    pl.semaphore_wait(barrier, len(partners))
-
-    far_copies = {}
-
-    def send_far(_):
-        for k in (1, 3, 2):
-            far_copies[k] = remote(far.at[0], far.at[k], far_s.at[k], far_r.at[k], along_z(4 * k))
-
-    for i in range(3, 6):
-        inputs[i].start()
-
     row, col = iota((512, 256), 0), iota((512, 256), 1)
     hop = row >> 7
     dz = jnp.where(hop == 0, 0, jnp.where(hop == 1, 1, jnp.where(hop == 2, NZ - 1, two)))
@@ -124,15 +118,35 @@
     def spread(block):
         return jnp.concatenate([block] * 8, axis=0).astype(BF16)
 
+    def select(k, out):
+        chosen = lax.dot_general(wanted[...], spread(turns(k, False)), nt, preferred_element_type=F32)
+        chosen = jnp.where(same_group, chosen, 0.0).astype(BF16)
+        out[...] = jnp.dot(chosen, far[k, 0:128, :], preferred_element_type=F32).astype(BF16)
+
+    select(0, picked[0])
+    pl.semaphore_wait(barrier, len(partners))
+
+    far_copies = {}
+
+    def send_far(_):
+        for k in (1, 3):
+            far_copies[k] = remote(far.at[0], far.at[k], far_s.at[k], far_r.at[k], along_z(4 * k))
+
+    def forward_far(_):
+        for k, rows, i in ((1, pl.ds(0, 80), 0), (3, pl.ds(80, 64), 2)):
+            far_copies[k].wait_recv()
+            far_copies[i] = remote(far.at[k, rows], far.at[2, rows], far_s.at[i], far_r.at[i], along_z(4 * k))
+
+    for i in range(3, 6):
+        inputs[i].start()
+
     def select_and_send(g):
         for i, k in enumerate(GROUPS[g]):
+            if k == 2:
+                far_copies[0].wait_recv()
+                far_copies[2].wait_recv()
             if k:
-                far_copies[k].wait_recv()
-            chosen = lax.dot_general(wanted[...], spread(turns(k, False)), nt, preferred_element_type=F32)
-            chosen = jnp.where(same_group, chosen, 0.0).astype(BF16)
-            picked[g][:, 128 * i : 128 * i + 128] = jnp.dot(
-                chosen, far[k, 0:128, :], preferred_element_type=F32
-            ).astype(BF16)
+                select(k, picked[g].at[:, pl.ds(128 * i, 128)])
         for j in range(NEAR - 1, 0, -1):
             remote(
                 picked[g].at[pl.ds(16 * j, 16)], got[g].at[pl.ds(16 * j, 16)],
@@ -168,9 +182,9 @@
                 xf[y, first : first + 64, 128 * group : 128 * group + 128] = rows[
                     64 * group : 64 * group + 64, 128 * i : 128 * i + 128
                 ]
-        block = xf.at[y, pl.ds(BASE[g], ROWS[g])]
-        y_copies[g, 0] = remote(block, block, y_s.at[g, 0], y_r.at[g, 0], along_y(1))
-        y_copies[g, 1] = remote(block, block, y_s.at[g, 1], y_r.at[g, 1], along_y(3))
+        for i, half, dy in ((0, first_half(g), 1), (1, second_half(g), 3), (4, second_half(g), 1), (5, first_half(g), 3)):
+            block = xf.at[y, half]
+            y_copies[g, i] = remote(block, block, y_s.at[g, i], y_r.at[g, i], along_y(dy))
 
     def first_half(g):
         return pl.ds(BASE[g], ROWS[g] // 2)
@@ -189,8 +203,8 @@
     def expert(which):
         members = EXPERT[which]
         for g in members:
-            y_copies[g, 2].wait_recv()
-            y_copies[g, 3].wait_recv()
+            for i in range(2, 6):
+                y_copies[g, i].wait_recv()
         count = sum(ROWS[g] for g in members)
         rows = pl.ds(BASE[members[0]], count)
         gate_out, up_out = jnp.zeros((count, 192), F32), jnp.zeros((count, 192), F32)
@@ -204,35 +218,40 @@
                 hidden, down[:, 1024 * q : 1024 * q + 1024], preferred_element_type=F32
             ).astype(BF16)
         opposite = lax.rem(y + 2, NY)
+        members = [g for g in members if g not in MIX]
         for g in members:
             for side, half, dy in ((0, first_half(g), 1), (1, second_half(g), 3)):
                 one_copies[g, side] = remote(
                     pf.at[opposite, half], step1.at[half], one_s.at[g, side], one_r.at[g, side], along_y(dy)
                 )
+        for g in members:
+            for side, half, dy in ((0, second_half(g), 1), (1, first_half(g), 3)):
+                two_copies[g, 2 + side] = remote(
+                    pf.at[lax.rem(y + dy, NY), half], step2.at[side, half],
+                    two_s.at[g, 2 + side], two_r.at[g, 2 + side], along_y(dy),
+                )
 
     def add_y(g):
         for side, half, dy in ((0, first_half(g), 1), (1, second_half(g), 3)):
             one_copies[g, side].wait_recv()
             to = lax.rem(y + dy, NY)
             pf[to, half, :] = (pf[to, half, :].astype(F32) + step1[half, :].astype(F32)).astype(BF16)
-            rows = pl.ds(BASE[g], ROWS[g])
             two_copies[g, side] = remote(
-                pf.at[to, rows], step2.at[side, rows], two_s.at[g, side], two_r.at[g, side], along_y(dy)
+                pf.at[to, half], step2.at[side, half], two_s.at[g, side], two_r.at[g, side], along_y(dy)
             )
 
+    def stack(total):
+        return jnp.concatenate([total[:, 128 * group : 128 * group + 128] for group in range(8)], axis=0)
+
     def give_back(g):
-        two_copies[g, 0].wait_recv()
-        two_copies[g, 1].wait_recv()
-        parts = []
-        for i in range(len(GROUPS[g])):
-            rows = pl.ds(BASE[g] + 64 * i, 64)
-            total = (
-                pf[y, rows, :].astype(F32) + step2[0, rows, :].astype(F32) + step2[1, rows, :].astype(F32)
-            ).astype(BF16)
-            parts.append(
-                jnp.concatenate([total[:, 128 * group : 128 * group + 128] for group in range(8)], axis=0)
-            )
-        stacked = jnp.concatenate(parts, axis=1) if len(parts) > 1 else parts[0]
+        rows = pl.ds(BASE[g], 64)
+        if g in MIX:
+            stacked = jnp.concatenate([stack(pf[q, rows, :]) for q in range(NY)], axis=1)
+        else:
+            for i in range(4):
+                two_copies[g, i].wait_recv()
+            total = pf[y, rows, :].astype(F32) + step2[0, rows, :].astype(F32) + step2[1, rows, :].astype(F32)
+            stacked = stack(total.astype(BF16))
         back_out[g][...] = jnp.dot(perm_back[...], stacked, preferred_element_type=F32).astype(BF16)
         for j in range(NEAR - 1, 0, -1):
             remote(
@@ -243,21 +262,41 @@
 
     own = []
 
+    def send_part(k, part):
+        part_out[k] = part.astype(BF16)
+        part_copies[k] = remote(
+            part_out.at[k], part_in.at[k], part_s.at[k], part_r.at[k], along_z(NZ - 4 * k)
+        )
+
     def combine(g):
         wait_all(back_in[g], back_r.at[g])
-        for i, k in enumerate(GROUPS[g]):
-            part = jnp.dot(weighted[k], back_in[g][:, 128 * i : 128 * i + 128], preferred_element_type=F32)
-            if k == 0:
-                own.append(part)
-            else:
-                part_out[k] = part.astype(BF16)
-                part_copies[k] = remote(
-                    part_out.at[k], part_in.at[k], part_s.at[k], part_r.at[k], along_z(NZ - 4 * k)
+        [k] = GROUPS[g]
+        part = jnp.dot(weighted[k], back_in[g][...], preferred_element_type=F32)
+        if g in MIX:
+            for q in range(NY):
+                all_out[g, q] = part[:, 128 * q : 128 * q + 128].astype(BF16)
+            for dy in (2, 1, 3):
+                all_copies[g, dy] = remote(
+                    all_out.at[g, lax.rem(y + dy, NY)], all_in.at[g, dy], all_s.at[g, dy], all_r.at[g, dy],
+                    along_y(dy),
                 )
+        elif k == 0:
+            own.append(part)
+        else:
+            send_part(k, part)
+
+    all_copies = {}
+
+    def sum_y(g):
+        part = all_out[g, y].astype(F32)
+        for dy in (1, 3, 2):
+            all_copies[g, dy].wait_recv()
+            part += all_in[g, dy].astype(F32)
+        send_part(GROUPS[g][0], part)
 
     stages = {
         "a": select_and_send, "p": permutations, "b": send_y, "c": forward_y, "w": weights,
-        "h": send_far, "d": expert, "e": add_y, "f": give_back, "g": combine,
+        "s": sum_y, "h": send_far, "i": forward_far, "d": expert, "e": add_y, "f": give_back, "g": combine,
     }
     for stage, g in ORDER:
         stages[stage](g)
@@ -272,21 +311,28 @@
     for g in range(len(GROUPS)):
         wait_all(picked[g], near_s.at[g])
         wait_all(back_out[g], back_s.at[g])
-        for i in range(4):
+        for i in range(6):
             y_copies[g, i].wait_send()
-        for i in range(2):
-            one_copies[g, i].wait_send()
-            two_copies[g, i].wait_send()
-    for k in range(1, 4):
+        if g in MIX:
+            for dy in (1, 2, 3):
+                all_copies[g, dy].wait_send()
+        else:
+            for i in range(2):
+                one_copies[g, i].wait_send()
+            for i in range(4):
+                two_copies[g, i].wait_send()
+    for k in range(4):
         far_copies[k].wait_send()
-        part_copies[k].wait_send()
+        if k:
+            part_copies[k].wait_send()
 
 
 def per_device(tokens, expert_ids, route_probs, gate_weight, up_weight, down_weight):
     vmem, dma = pltpu.VMEM, pltpu.SemaphoreType.DMA
     in_hbm = pl.BlockSpec(memory_space=pltpu.HBM)
     n = len(GROUPS)
-    messages = [vmem((512, 128 * len(members)), BF16) for members in GROUPS]
+    ahead = [vmem((512, 128), BF16)] * n
+    back = [vmem((512, 512 if g in MIX else 128), BF16) for g in range(n)]
     return pl.pallas_call(
         kernel,
         out_shape=jax.ShapeDtypeStruct((16, 1024), BF16),
@@ -302,9 +348,9 @@
             vmem((256, 1024), BF16), vmem((2, 256, 1024), BF16),
             vmem((4, 128, 128), BF16), vmem((4, 128, 128), BF16),
             dma((6,)), dma((4,)), dma((4,)), dma((n,)), dma((n,)),
-            dma((n, 4)), dma((n, 4)), dma((n, 2)), dma((n, 2)), dma((n, 2)), dma((n, 2)),
+            dma((n, 6)), dma((n, 6)), dma((n, 2)), dma((n, 2)), dma((n, 4)), dma((n, 4)),
             dma((n,)), dma((n,)), dma((4,)), dma((4,)),
-        ] + messages * 4,
+        ] + ahead * 2 + back * 2 + [vmem((n, 4, 128, 128), BF16)] * 2 + [dma((n, 4))] * 2,
         compiler_params=pltpu.CompilerParams(
             collective_id=0, has_side_effects=True, vmem_limit_bytes=60 * 1024 * 1024
         ),

time: 80.1 us -> 77.3 us (0.965)
  Pallas kernels: 78.4 us -> 75.7 us
    pallas_call x1, Pallas kernels: 78.4 us -> 75.7 us  [per_device(): pl.pallas_call(kernel, out_shape=jax.ShapeDtypeStruct((16, 1024), BF16),...]
where the time goes in v2:
time: 77.3 us; the launch traced here: 77.1 us
  Pallas kernels  75.7 us (98%)
  local copies, waits for them, and re-layouts  1.38 us (2%)
    pallas_call x1, Pallas kernels, per_device(): pl.pallas_call(kernel, out_shape=jax.ShapeDtypeStruct((16, 1024), BF16),...  75.7 us

profile of v2, /device:TPU:1, one launch (start us, length us, event | category | flops | bytes accessed | tf_op | source)
XLA Modules:
  0.0 77.1 jit_solution(17635466480411607620)
XLA Ops:
  0.0 75.7 %shard_map.64 = bf16[16,1024]{1,0:T(8,128)(2,1)} custom-call(bf16[16,1024]{1,0:T(8,128)(2,1)} %tok_hbm.1, s32[8,16]{1,0:T(8,128)} %bitcast.2, f32[8,16]{1,0:T(8,128)} %bitcast.3, bf16[1,192,4096]{2,1,0:T(8,128)(2,1)} %gate_hbm.1, bf16[1,192,4096]{2,1,0:T(8,128)(2,1)} %up_hbm.1, bf16[1,192,4096]{2,1,0:T(8,128)(2,1)} %down_hbm.1), custom_call_target="tpu_custom_call" | custom-call | flops 1300000000 | bytes 5000000 | tf_op jit(solution)/shard_map/pallas_call | solution.py:336
  75.7 1.4 %copy.8 = bf16[16,1024]{1,0:T(8,128)(2,1)} copy(bf16[16,1024]{1,0:T(8,128)(2,1)} %shard_map.64) | data formatting | bytes 65536

commit v3 on v2

--- a/solution.py
+++ b/solution.py
@@ -16,9 +16,9 @@
 EXPERT = ((0,), (1,), (2,), (3,))
 MIX = (2,)
 ORDER = (
-    ("h", 0), ("a", 0), ("p", 0), ("b", 0), ("i", 0), ("a", 1), ("a", 2), ("c", 0), ("b", 1), ("a", 3),
+    ("h", 0), ("a", 0), ("p", 0), ("i", 0), ("a", 1), ("b", 0), ("a", 2), ("c", 0), ("b", 1), ("a", 3),
     ("b", 2), ("c", 1), ("w", 0), ("b", 3), ("c", 2), ("d", 1), ("c", 3), ("d", 2), ("f", 2), ("e", 1),
-    ("d", 3), ("f", 1), ("d", 0), ("e", 3), ("g", 2), ("e", 0), ("g", 1), ("s", 2), ("f", 3), ("f", 0),
+    ("d", 3), ("d", 0), ("e", 3), ("f", 1), ("e", 0), ("g", 2), ("g", 1), ("s", 2), ("f", 3), ("f", 0),
     ("g", 3), ("g", 0),
 )
 

time: 77.3 us -> 77.2 us (level)
  no operation moved by 1% of the time
where the time goes in v3:
time: 77.2 us; the launch traced here: 77 us
  Pallas kernels  75.6 us (98%)
  local copies, waits for them, and re-layouts  1.38 us (2%)
    pallas_call x1, Pallas kernels, per_device(): pl.pallas_call(kernel, out_shape=jax.ShapeDtypeStruct((16, 1024), BF16),...  75.6 us

profile of v3, /device:TPU:1, one launch (start us, length us, event | category | flops | bytes accessed | tf_op | source)
XLA Modules:
  0.0 77.0 jit_solution(3615738846716692360)
XLA Ops:
  0.0 75.6 %shard_map.64 = bf16[16,1024]{1,0:T(8,128)(2,1)} custom-call(bf16[16,1024]{1,0:T(8,128)(2,1)} %tok_hbm.1, s32[8,16]{1,0:T(8,128)} %bitcast.2, f32[8,16]{1,0:T(8,128)} %bitcast.3, bf16[1,192,4096]{2,1,0:T(8,128)(2,1)} %gate_hbm.1, bf16[1,192,4096]{2,1,0:T(8,128)(2,1)} %up_hbm.1, bf16[1,192,4096]{2,1,0:T(8,128)(2,1)} %down_hbm.1), custom_call_target="tpu_custom_call" | custom-call | flops 1300000000 | bytes 5000000 | tf_op jit(solution)/shard_map/pallas_call | solution.py:336
  75.6 1.4 %copy.8 = bf16[16,1024]{1,0:T(8,128)(2,1)} copy(bf16[16,1024]{1,0:T(8,128)(2,1)} %shard_map.64) | data formatting | bytes 65536
